TPU v7x, 32 devices: a whole 2x2x4 slice. The times are simulated.
32 devices in a mesh: mem: 4 (over y, core), gx: 8 (over z, x).
Axes of the slice: x: 2, y: 2, z: 4, core: 2. Of those that a mesh axis runs over, the one named last changes fastest.
Arguments:
- weights: bfloat16 [4, 128, 32768], P('mem', 'gx'), may hold values from -6 to 6
- perturbations: bfloat16 [2, 4, 128, 32768], P(None, 'mem', 'gx'), may hold values from -3 to 3
- obs_cell: int32 [32768], P('gx'), may hold values from 0 to 524287
- obs_slot: int32 [32768], P('gx'), may hold values from 0 to 1
- innovation: float32 [32768], P('gx'), may hold values from -24 to 24
- obs_weight: float32 [32768], P('gx'), may hold values from 0.5 to 4
- obs_count: int32 [8], P('gx'), may hold values from 2048 to 4096, as said below
Outputs:
- gradient: float32 [4, 128, 32768], P('mem', 'gx')
Inputs may be any that keep to these rules, and one draw needn't show every extreme that they name: Slab s uses its first obs_count[s] observation slots, o = s * 4096 .. s * 4096 + obs_count[s] - 1; some slab is full and another holds 2048. `obs_cell`: the cell is numbered (x within the slab) * 512 * 64 + y * 64 + z; several observations may share a cell.
All inputs are finite; a program needn't handle non-finite values.
Results may differ from a plain program's by a relative error of at most 0.0029.
Values may be sent and summed in bfloat16 or wider, within the bound.
A program may use at most 64 MiB of HBM per device.

v0:
```python
import jax
import jax.numpy as jnp
from jax import lax
from jax.sharding import PartitionSpec as P

NY = 512
NZ = 64


tap_reach = 15
corr_scale = 7.0


def padded_2(block, sides, width):
    for axis, dim in sides:
        count = lax.axis_size(axis)
        forward = [(i, i + 1) for i in range(count - 1)]
        backward = [(target, source) for source, target in forward]
        low = lax.ppermute(
            lax.slice_in_dim(block, block.shape[dim] - width, None, axis=dim), axis, forward
        )
        high = lax.ppermute(lax.slice_in_dim(block, 0, width, axis=dim), axis, backward)
        block = jnp.concatenate([low, block, high], axis=dim)
    return block


def tap_values():
    offsets = jnp.arange(-tap_reach, tap_reach + 1).astype(jnp.float32)
    bell = jnp.exp(-offsets * offsets / (2.0 * corr_scale * corr_scale))
    return (bell / jnp.sqrt(jnp.sum(bell * bell))).astype(jnp.bfloat16)


def band_matrix(count_out, count_in, start):
    out_pos = jnp.arange(count_out)
    in_pos = jnp.arange(count_in)
    offsets = in_pos[None, :] - out_pos[:, None] - start
    tap_table = tap_values()
    lookup = tap_table[jnp.clip(offsets + tap_reach, 0, 2 * tap_reach)]
    return jnp.where(jnp.abs(offsets) <= tap_reach, lookup, jnp.zeros_like(lookup))


def along_z(field):
    members, slab_rows, plane_cells = field.shape
    band_z = band_matrix(NZ, NZ, 0)
    grid = field.reshape(members, slab_rows, NY, NZ)
    result = jnp.einsum("mxyq,zq->mxyz", grid, band_z, preferred_element_type=jnp.float32)
    return result.reshape(members, slab_rows, plane_cells)


def along_y(field):
    members, slab_rows, plane_cells = field.shape
    band_y = band_matrix(NY, NY, 0)
    grid = field.reshape(members, slab_rows, NY, NZ)
    result = jnp.einsum("mxqz,yq->mxyz", grid, band_y, preferred_element_type=jnp.float32)
    return result.reshape(members, slab_rows, plane_cells)


def along_x(padded, slab_rows):
    band_x = band_matrix(slab_rows, slab_rows + 2 * tap_reach, tap_reach)
    return jnp.einsum("ip,mpc->mic", band_x, padded, preferred_element_type=jnp.float32)


def local(weights, perturbations, obs_cell, obs_slot, innovation, obs_weight, obs_count):
    members, slab_rows, plane_cells = weights.shape
    slot_count = perturbations.shape[0]
    z_smooth = along_z(weights).astype(jnp.bfloat16)
    y_smooth = along_y(z_smooth).astype(jnp.bfloat16)
    padded = padded_2(y_smooth, (("gx", 1),), tap_reach)
    smoothed = along_x(padded, slab_rows)
    partial_sum = jnp.sum(perturbations.astype(jnp.float32) * smoothed[None], axis=1)
    increment = lax.psum(partial_sum, "mem")
    flat_increment = increment.reshape(slot_count, slab_rows * plane_cells)
    sampled = flat_increment[obs_slot, obs_cell]
    live_mask = (jnp.arange(obs_cell.shape[0]) < obs_count[0]).astype(jnp.float32)
    residual = live_mask * obs_weight * (sampled - innovation)
    forcing = (
        jnp.zeros((slot_count, slab_rows * plane_cells), jnp.float32)
        .at[obs_slot, obs_cell]
        .add(residual)
    )
    forcing = forcing.reshape(slot_count, 1, slab_rows, plane_cells)
    adjoint_source = jnp.sum(perturbations.astype(jnp.float32) * forcing, axis=0).astype(
        jnp.bfloat16
    )
    padded_back = padded_2(adjoint_source, (("gx", 1),), tap_reach)
    x_back = along_x(padded_back, slab_rows).astype(jnp.bfloat16)
    y_back = along_y(x_back).astype(jnp.bfloat16)
    return weights.astype(jnp.float32) + along_z(y_back)


def solution(mesh):
    return jax.shard_map(
        local,
        mesh=mesh,
        in_specs=(
            P("mem", "gx", None),
            P(None, "mem", "gx", None),
            P("gx"),
            P("gx"),
            P("gx"),
            P("gx"),
            P("gx"),
        ),
        out_specs=P("mem", "gx", None),
        check_vma=False,
    )
```

profile of v0, /device:TPU:0, one launch (start us, length us, event | category | flops | bytes accessed | tf_op | source)
XLA Modules:
  0.0 381.5 jit_solution(5355239928933844779)
XLA Ops:
  6.5 0.6 multiply_reduce_fusion.1
  7.9 0.7 fusion.197
  8.6 0.7 fusion.198
  9.4 24.4 %gather_fusion = bf16[4096]{0:T(1024)(128)(2,1)S(1)} fusion(bf16[31]{0:T(256)(128)(2,1)S(1)} %divide_convert_fusion, s32[4096]{0:T(1024)S(1)} %broadcast_clamp_fusion), kind=kCustom, calls=%fused_computation | custom fusion | bytes 32768 | tf_op jit(solution)/shard_map/gather | solution.py:38
  33.9 2.3 reshape.170
  36.2 0.8 convolution_convert_fusion.1
  37.1 22.6 %fusion.104 = f32[512,1024]{0,1:S(1)} fusion(bf16[512,1024]{0,1:T(8,128)(2,1)S(1)} %bitcast.898, bf16[]{:T(256)} %bitcast.48, bf16[]{:T(256)} %bitcast.49, bf16[]{:T(256)} %bitcast.50, bf16[]{:T(256)} %bitcast.51, bf16[]{:T(256)} %bitcast.52, bf16[]{:T(256)} %bitcast.54, bf16[]{:T(256)} %bitcast.53, bf16[]{:T(256)} %bitcast.1, bf16[]{:T(256)} %bitcast.3, ...), kind=kOutput, calls=%fused_computation.119 | convolution fusion | flops 555220992 | bytes 3145790
  59.8 1.1 copy.9
  60.9 1.7 convert_element_type.100
  62.6 1.5 fusion.196
  64.1 5.8 %collective-permute-start = (bf16[1,15,32768]{2,1,0:T(8,128)(2,1)}, bf16[1,15,32768]{2,1,0:T(8,128)(2,1)}, u32[]{:S(2)}, u32[]{:S(2)}) collective-permute-start(bf16[1,15,32768]{2,1,0:T(8,128)(2,1)} %get-tuple-element.7), channel_id=1, source_target_pairs={{0,1},{1,2},{2,3},{3,4},{4,5},{5,6},{6,7},{8,9},{9,10},{10,11},{11... | collective-permute-start | bytes 2949128 | tf_op jit(solution)/shard_map/ppermute | solution.py:19
  70.0 1.5 collective-permute-start.1
  71.6 4.8 %gather_fusion.1 = bf16[736]{0:T(1024)(128)(2,1)S(1)} fusion(bf16[31]{0:T(256)(128)(2,1)S(1)} %divide_convert_fusion, s32[1024]{0:T(1024)S(1)} %pad_clamp_fusion), kind=kCustom, calls=%fused_computation.1 | custom fusion | bytes 5888 | tf_op jit(solution)/shard_map/gather | solution.py:38
  76.4 37.7 %collective-permute-done = bf16[1,15,32768]{2,1,0:T(8,128)(2,1)} collective-permute-done((bf16[1,15,32768]{2,1,0:T(8,128)(2,1)}, bf16[1,15,32768]{2,1,0:T(8,128)(2,1)}, u32[]{:S(2)}, u32[]{:S(2)}) %collective-permute-start) | collective-permute-done | bytes 983072 | tf_op jit(solution)/shard_map/ppermute | solution.py:19
  114.2 2.5 convolution_bitcast_fusion
  116.7 0.3 fusion.1
  117.0 5.2 %copy.13 = f32[1,2,16,32768]{3,1,2,0:T(2,128)} copy(f32[1,2,16,32768]{3,2,1,0:T(8,128)S(1)} %fusion.1) | data formatting | bytes 8388608
  123.3 86.8 %all-reduce.2.cloned.1.call-done = f32[2,524288]{1,0:T(2,128)} async-done(((f32[2,524288]{1,0:T(2,128)}), f32[2,524288]{1,0:T(2,128)}) %all-reduce.2.cloned.1.call-update) | async-done | bytes 4194320 | tf_op jit(solution)/shard_map/psum | solution.py:71
  210.1 50.3 %gather_fusion.2 = f32[4096]{0:T(1024)S(1)} fusion(f32[2,524288]{1,0:T(2,128)} %all-reduce.2.cloned.1.call-done, s32[4096]{0:T(1024)S(1)} %bitcast.891), kind=kCustom, calls=%fused_computation.2 | custom fusion | bytes 65536 | tf_op jit(solution)/shard_map/gather | solution.py:73
  260.5 24.1 %scatter_custom_fusion = f32[1048576]{0:T(1024)} fusion(s32[4096]{0:T(1024)S(1)} %broadcast_select_fusion, f32[4096]{0:T(1024)S(1)} %subtract_multiply_fusion, f32[]{:T(128)} %constant.13.clone.1), kind=kCustom, calls=%fused_computation.22 | custom fusion | flops 4096 | bytes 4194308
  284.6 5.0 %reshape.173 = f32[2,1,16,32768]{3,2,1,0:T(8,128)} reshape(f32[1048576]{0:T(1024)} %scatter_custom_fusion) | data formatting | bytes 8388608 | tf_op jit(solution)/shard_map/reshape | solution.py:81
  289.6 2.8 fusion.2
  292.6 3.4 collective-permute-start.2
  296.0 1.5 collective-permute-start.3
  297.5 43.1 %collective-permute-done.2 = bf16[1,15,32768]{2,1,0:T(8,128)(2,1)S(1)} collective-permute-done((bf16[1,15,32768]{2,1,0:T(8,128)(2,1)S(1)}, bf16[1,15,32768]{2,1,0:T(8,128)(2,1)S(1)}, u32[]{:S(2)}, u32[]{:S(2)}) %collective-permute-start.2) | collective-permute-done | bytes 983072 | tf_op jit(solution)/shard_map/ppermute | solution.py:19
  340.6 1.0 fusion
  341.7 2.3 reshape.175
  344.0 0.8 copy.10
  344.8 22.6 %fusion.102 = f32[512,1024]{0,1:S(1)} fusion(bf16[512,1024]{0,1:T(8,128)(2,1)S(1)} %bitcast.897, bf16[]{:T(256)} %bitcast.48, bf16[]{:T(256)} %bitcast.49, bf16[]{:T(256)} %bitcast.50, bf16[]{:T(256)} %bitcast.51, bf16[]{:T(256)} %bitcast.52, bf16[]{:T(256)} %bitcast.54, bf16[]{:T(256)} %bitcast.53, bf16[]{:T(256)} %bitcast.1, bf16[]{:T(256)} %bitcast.3, ...), kind=kOutput, calls=%fused_computation.118 | convolution fusion | flops 555220992 | bytes 3145790
  367.4 2.7 fusion.13
  370.1 3.0 reshape.177
  373.1 1.5 convert_add_fusion
  (40 shorter events, 1.1 us)
Async XLA Ops:
  6.5 203.6 %all-reduce.2.cloned.1.call-start = ((), (), s32[]{:S(2)}) async-start(), calls=%async_computation | async-start | bytes 8388608 | tf_op jit(solution)/shard_map/psum | solution.py:71
  9.4 24.5 %copy-start.1 = (bf16[1,16,32768]{2,1,0:T(8,128)(2,1)S(1)}, bf16[1,16,32768]{2,1,0:T(8,128)(2,1)}, u32[]{:S(2)}) copy-start(bf16[1,16,32768]{2,1,0:T(8,128)(2,1)} %param.7) | copy-start | bytes 3145732
  64.1 50.0 %collective-permute-start = (bf16[1,15,32768]{2,1,0:T(8,128)(2,1)}, bf16[1,15,32768]{2,1,0:T(8,128)(2,1)}, u32[]{:S(2)}, u32[]{:S(2)}) collective-permute-start(bf16[1,15,32768]{2,1,0:T(8,128)(2,1)} %get-tuple-element.7), channel_id=1, source_target_pairs={{0,1},{1,2},{2,3},{3,4},{4,5},{5,6},{6,7},{8,9},{9,10},{10,11},{11... | collective-permute-start | bytes 2949128 | tf_op jit(solution)/shard_map/ppermute | solution.py:19
  70.0 44.2 %collective-permute-start.1 = (bf16[1,15,32768]{2,1,0:T(8,128)(2,1)}, bf16[1,15,32768]{2,1,0:T(8,128)(2,1)}, u32[]{:S(2)}, u32[]{:S(2)}) collective-permute-start(bf16[1,15,32768]{2,1,0:T(8,128)(2,1)} %get-tuple-element.8), channel_id=1, source_target_pairs={{1,0},{2,1},{3,2},{4,3},{5,4},{6,5},{7,6},{9,8},{10,9},{11,10},{12... | collective-permute-start | bytes 2949128 | tf_op jit(solution)/shard_map/ppermute | solution.py:22
  76.4 40.2 %copy-start = (bf16[2,1,16,32768]{3,2,1,0:T(8,128)(2,1)S(1)}, bf16[2,1,16,32768]{3,2,1,0:T(8,128)(2,1)}, u32[]{:S(2)}) copy-start(bf16[2,1,16,32768]{3,2,1,0:T(8,128)(2,1)} %param.8) | copy-start | bytes 6291460
  122.2 0.7 copy-start.3
  122.2 0.7 copy-start.4
  122.2 0.8 copy-start.7
  122.2 0.9 copy-start.8
  210.1 50.4 %copy-start.5 = (f32[4096]{0:T(1024)S(1)}, f32[4096]{0:T(1024)}, u32[]{:S(2)}) copy-start(f32[4096]{0:T(1024)} %param.11) | copy-start | bytes 49156
  210.1 50.4 %copy-start.6 = (f32[4096]{0:T(1024)S(1)}, f32[4096]{0:T(1024)}, u32[]{:S(2)}) copy-start(f32[4096]{0:T(1024)} %param.12) | copy-start | bytes 49156
  292.6 48.1 %collective-permute-start.2 = (bf16[1,15,32768]{2,1,0:T(8,128)(2,1)S(1)}, bf16[1,15,32768]{2,1,0:T(8,128)(2,1)S(1)}, u32[]{:S(2)}, u32[]{:S(2)}) collective-permute-start(bf16[1,15,32768]{2,1,0:T(8,128)(2,1)S(1)} %get-tuple-element.5), channel_id=1, source_target_pairs={{0,1},{1,2},{2,3},{3,4},{4,5},{5,6},{6,7},{8,9},{9,10},{10,11},{11... | collective-permute-start | bytes 2949128 | tf_op jit(solution)/shard_map/ppermute | solution.py:19
  296.0 44.7 %collective-permute-start.3 = (bf16[1,15,32768]{2,1,0:T(8,128)(2,1)S(1)}, bf16[1,15,32768]{2,1,0:T(8,128)(2,1)S(1)}, u32[]{:S(2)}, u32[]{:S(2)}) collective-permute-start(bf16[1,15,32768]{2,1,0:T(8,128)(2,1)S(1)} %get-tuple-element.6), channel_id=1, source_target_pairs={{1,0},{2,1},{3,2},{4,3},{5,4},{6,5},{7,6},{9,8},{10,9},{11,10},{12... | collective-permute-start | bytes 2949128 | tf_op jit(solution)/shard_map/ppermute | solution.py:22
  370.1 3.0 copy-start.2
Sparse Core Ops, SparseCore 0:
  122.4 87.6 all-reduce.1
where the time goes:
time: 384 us; the launch traced here: 381 us
  waiting for transfers between devices  168 us (44%)
  local copies, waits for them, and re-layouts  104 us (27%)
  matrix products  52.2 us (14%)
  other arithmetic  29.8 us (8%)
  between operations  15.1 us (4%)
  starting transfers between devices  12.2 us (3%)
    psum x1, waiting for transfers between devices, local(): increment = lax.psum(partial_sum, 'mem')  86.8 us
    ppermute x2, waiting for transfers between devices, padded_2(): lax.ppermute(lax.slice_in_dim(block, block.shape[dim] - width, None, axis...  80.8 us
    gather x1, local copies, waits for them, and re-layouts, local(): sampled = flat_increment[obs_slot, obs_cell]  50.3 us
    unnamed x2, matrix products  45.1 us
    gather x6, local copies, waits for them, and re-layouts, band_matrix(): lookup = tap_table[jnp.clip(offsets + tap_reach, 0, 2 * tap_reach)]  30.8 us
    unnamed x5, other arithmetic  24.6 us
    ppermute x2, starting transfers between devices, padded_2(): lax.ppermute(lax.slice_in_dim(block, block.shape[dim] - width, None, axis...  9.24 us
  transfers between devices with their start and end apart: 5, of which 3 were waited for; matrix products, arithmetic and copies ran while one was open for 1% of the time, Pallas kernels for 0%

commit v1 on v0

v1 whole, which is shorter than its diff:
```python
import functools

import ml_dtypes
import numpy as np

import jax
import jax.numpy as jnp
from jax import lax
from jax.experimental import pallas as pl
from jax.experimental.pallas import tpu as pltpu
from jax.sharding import PartitionSpec as P

NY = 512
NZ = 64
REACH = 15
LANES = 128
PAIRS = NY // 2
LOW = 64
HIGH = PAIRS // LOW
VMEM_LIMIT = 56 * 1024 * 1024
NT = (((1,), (1,)), ((), ()))


def tap_values():
    j = np.arange(-REACH, REACH + 1).astype(np.float32)
    bell = np.exp(-j * j / np.float32(98.0))
    return (bell / np.sqrt(np.sum(bell * bell))).astype(ml_dtypes.bfloat16)


def taps_at(offset):
    taps = tap_values()
    look = taps[np.clip(offset + REACH, 0, 2 * REACH)]
    return np.where(np.abs(offset) <= REACH, look, np.zeros_like(look))


def z_band():
    z = np.arange(LANES) % NZ
    half = np.arange(LANES) // NZ
    band = taps_at(z[:, None] - z[None, :])
    return np.where(half[:, None] == half[None, :], band, np.zeros_like(band))


def y_band(rows):
    out_c, out_x = np.arange(16 * rows) // rows, np.arange(16 * rows) % rows
    in_c, in_x = np.arange(32 * rows) // rows - 8, np.arange(32 * rows) % rows
    step = 2 * (in_c[None, :] - out_c[:, None])
    same = out_x[:, None] == in_x[None, :]
    parts = []
    for shift in (0, 1, -1):
        band = taps_at(step + shift)
        parts.append(np.where(same, band, np.zeros_like(band)))
    return np.concatenate(parts, axis=1)


def x_bands(rows):
    x = np.arange(rows)
    return np.stack([taps_at(x[:, None] - (x[None, :] + off)) for off in (0, -rows, rows)])


def split_cell(cell):
    x = cell >> 15
    pair = (cell >> 7) & (PAIRS - 1)
    low = pair & (LOW - 1)
    row = (pair // LOW) * LANES + (cell & (LANES - 1))
    return x, low, row


def fill_a(a_ref, x_rows, low, rows):
    count = x_rows.shape[1]
    low_b = jnp.broadcast_to(low.astype(jnp.float32), (rows, count)).astype(jnp.bfloat16)
    zero = jnp.zeros_like(x_rows)
    for c in range(LOW):
        a_ref[c * rows:(c + 1) * rows, :] = jnp.where(low_b == jnp.bfloat16(c), x_rows, zero)


def x_taps(kx, x, rows):
    hot = (lax.broadcasted_iota(jnp.int32, (rows, x.shape[1]), 0) == x)
    hot = hot.astype(jnp.float32).astype(jnp.bfloat16)
    if kx is None:
        return hot
    return jnp.dot(kx, hot, preferred_element_type=jnp.float32).astype(jnp.bfloat16)


def pairs_block(w_ref, b, rows):
    parts = []
    for j in range(16):
        start = pl.multiple_of((b * 16 + j) * LANES, LANES)
        parts.append(w_ref[:, pl.ds(start, LANES)])
    return jnp.concatenate(parts, axis=0)


def sample_kernel(block, w_ref, cell_ref, kz_ref, kyt_ref, kx_ref, s_ref, z_ref, y_ref, a_ref):
    rows = w_ref.shape[0]
    span = 16 * rows
    pad = 8 * rows
    depth = LOW * rows
    z_ref[:, :pad] = jnp.zeros((LANES, pad), jnp.bfloat16)
    z_ref[:, pad + PAIRS * rows:] = jnp.zeros((LANES, pad), jnp.bfloat16)

    @pl.loop(0, PAIRS // 16)
    def _(b):
        part = pairs_block(w_ref, b, rows)
        z = lax.dot_general(kz_ref[...], part, NT, preferred_element_type=jnp.float32)
        z_ref[:, pl.ds(pl.multiple_of(pad + b * span, LANES), span)] = z.astype(jnp.bfloat16)

    @pl.loop(0, PAIRS // 16)
    def _(b):
        win = z_ref[:, pl.ds(pl.multiple_of(b * span, LANES), 2 * span)]
        top, bottom = win[:NZ], win[NZ:]
        none = jnp.zeros_like(top)
        from_bottom = jnp.concatenate([bottom, none], axis=0)
        from_top = jnp.concatenate([none, top], axis=0)
        wide = jnp.concatenate([win, from_bottom, from_top], axis=1)
        y = jnp.dot(wide, kyt_ref[...], preferred_element_type=jnp.float32)
        high = b // (LOW // 16)
        col = pl.multiple_of((b % (LOW // 16)) * span, LANES)
        y_ref[pl.ds(pl.multiple_of(high * LANES, LANES), LANES), pl.ds(col, span)] = y.astype(
            jnp.bfloat16)

    per_list = cell_ref.shape[1] // 3

    @pl.loop(0, cell_ref.shape[1] // block)
    def _(i):
        at = pl.ds(pl.multiple_of(i * block, block), block)
        x, low, row = split_cell(cell_ref[:, at])
        kx = kx_ref[i // (per_list // block)]
        fill_a(a_ref, x_taps(kx, x, rows), low, rows)
        m = jnp.dot(y_ref[...], a_ref[...], preferred_element_type=jnp.float32)
        hit = lax.broadcasted_iota(jnp.int32, m.shape, 0) == row
        s_ref[:, at] = jnp.sum(jnp.where(hit, m, 0.0), axis=0, keepdims=True)


def pick_kernel(block, p_ref, cell_ref, slot_ref, eye_ref, o_ref, t_ref, a_ref):
    slots, rows = p_ref.shape[:2]
    span = 16 * rows

    for t in range(slots):
        @pl.loop(0, PAIRS // 16)
        def _(b):
            part = pairs_block(p_ref.at[t], b, rows)
            z = lax.dot_general(eye_ref[...], part, NT, preferred_element_type=jnp.float32)
            high = b // (LOW // 16)
            col = pl.multiple_of((b % (LOW // 16)) * span, LANES)
            row0 = pl.multiple_of((t * HIGH + high) * LANES, LANES)
            t_ref[pl.ds(row0, LANES), pl.ds(col, span)] = z.astype(jnp.bfloat16)

    @pl.loop(0, cell_ref.shape[1] // block)
    def _(i):
        at = pl.ds(pl.multiple_of(i * block, block), block)
        x, low, row = split_cell(cell_ref[:, at])
        row = row + slot_ref[:, at] * (HIGH * LANES)
        fill_a(a_ref, x_taps(None, x, rows), low, rows)
        m = jnp.dot(t_ref[...], a_ref[...], preferred_element_type=jnp.float32)
        hit = lax.broadcasted_iota(jnp.int32, m.shape, 0) == row
        o_ref[:, at] = jnp.sum(jnp.where(hit, m, 0.0), axis=0, keepdims=True)


def back_kernel(block, w_ref, cell_ref, v_ref, kz_ref, ky_ref, kx_ref, out_ref,
                g_ref, x_ref, a_ref, b_ref):
    rows = w_ref.shape[0]
    span = 16 * rows
    pad = 8 * rows
    depth = LOW * rows
    per_list = cell_ref.shape[1] // 3
    g_ref[...] = jnp.zeros_like(g_ref)

    @pl.loop(0, cell_ref.shape[1] // block)
    def _(i):
        at = pl.ds(pl.multiple_of(i * block, block), block)
        x, low, row = split_cell(cell_ref[:, at])
        kx = kx_ref[i // (per_list // block)]
        fill_a(a_ref, x_taps(kx, x, rows), low, rows)
        shape = (HIGH * LANES, block)
        hit = lax.broadcasted_iota(jnp.int32, shape, 0) == row
        b_ref[...] = jnp.where(hit, v_ref[:, at], 0.0).astype(jnp.bfloat16)
        g_ref[...] += lax.dot_general(
            a_ref[...], b_ref[...], NT, preferred_element_type=jnp.float32)

    x_ref[:pad, :] = jnp.zeros((pad, LANES), jnp.bfloat16)
    x_ref[pad + PAIRS * rows:, :] = jnp.zeros((pad, LANES), jnp.bfloat16)
    for h in range(HIGH):
        x_ref[pad + h * depth:pad + (h + 1) * depth, :] = g_ref[
            :, h * LANES:(h + 1) * LANES].astype(jnp.bfloat16)

    @pl.loop(0, PAIRS // 16)
    def _(b):
        win = x_ref[pl.ds(pl.multiple_of(b * span, LANES), 2 * span), :]
        first, second = win[:, :NZ], win[:, NZ:]
        none = jnp.zeros_like(first)
        from_second = jnp.concatenate([second, none], axis=1)
        from_first = jnp.concatenate([none, first], axis=1)
        tall = jnp.concatenate([win, from_second, from_first], axis=0)
        y = jnp.dot(ky_ref[...], tall, preferred_element_type=jnp.float32)
        z = jnp.dot(y.astype(jnp.bfloat16), kz_ref[...], preferred_element_type=jnp.float32)
        for j in range(16):
            lane = pl.ds(pl.multiple_of((b * 16 + j) * LANES, LANES), LANES)
            out_ref[:, lane] = z[j * rows:(j + 1) * rows] + w_ref[:, lane].astype(jnp.float32)


def vmem(count):
    return [pl.BlockSpec(memory_space=pltpu.VMEM)] * count


def local(weights, perturbations, obs_cell, obs_slot, innovation, obs_weight, obs_count):
    rows, plane = weights.shape[1:]
    slots = perturbations.shape[0]
    count = obs_cell.shape[0]
    w = weights[0]
    pert = perturbations[:, 0]
    depth = LOW * rows
    wide = HIGH * LANES
    padded = (PAIRS + 16) * rows
    params = pltpu.CompilerParams(vmem_limit_bytes=VMEM_LIMIT)
    bf16 = jnp.bfloat16

    slabs = lax.axis_size("gx")
    forward = [(i, i + 1) for i in range(slabs - 1)]
    backward = [(b, a) for a, b in forward]

    kz = jnp.asarray(z_band())
    ky_np = y_band(rows)
    ky, kyt = jnp.asarray(ky_np), jnp.asarray(np.ascontiguousarray(ky_np.T))
    kx = jnp.asarray(x_bands(rows))
    eye = jnp.asarray(np.eye(LANES).astype(ml_dtypes.bfloat16))

    cell_left = lax.ppermute(obs_cell, "gx", forward)
    cell_right = lax.ppermute(obs_cell, "gx", backward)
    cell = obs_cell.reshape(1, count)
    slot = obs_slot.reshape(1, count)
    cells = jnp.concatenate([obs_cell, cell_left, cell_right]).reshape(1, 3 * count)

    block = 512
    picked = pl.pallas_call(
        functools.partial(pick_kernel, block),
        out_shape=jax.ShapeDtypeStruct((1, count), jnp.float32),
        in_specs=vmem(4),
        out_specs=vmem(1)[0],
        scratch_shapes=[
            pltpu.VMEM((slots * wide, depth), bf16),
            pltpu.VMEM((depth, block), bf16),
        ],
        compiler_params=params,
        cost_estimate=pl.CostEstimate(
            flops=2 * slots * rows * plane * count, bytes_accessed=4 * rows * plane,
            transcendentals=0),
        name="pick",
    )(pert, cell, slot, eye)

    sampled3 = pl.pallas_call(
        functools.partial(sample_kernel, block),
        out_shape=jax.ShapeDtypeStruct((1, 3 * count), jnp.float32),
        in_specs=vmem(5),
        out_specs=vmem(1)[0],
        scratch_shapes=[
            pltpu.VMEM((LANES, padded), bf16),
            pltpu.VMEM((wide, depth), bf16),
            pltpu.VMEM((depth, block), bf16),
        ],
        compiler_params=params,
        cost_estimate=pl.CostEstimate(
            flops=6 * rows * plane * count, bytes_accessed=2 * rows * plane, transcendentals=0),
        name="sample",
    )(w, cells, kz, kyt, kx)[0]
    own, for_left, for_right = sampled3[:count], sampled3[count:2 * count], sampled3[2 * count:]
    own = own + lax.ppermute(for_left, "gx", backward) + lax.ppermute(for_right, "gx", forward)

    picked = picked[0]
    share = picked * own
    members = lax.axis_size("mem")
    sampled = share
    for step in range(1, members):
        sampled = sampled + lax.ppermute(
            share, "mem", [(i, (i + step) % members) for i in range(members)])
    live_mask = (jnp.arange(count) < obs_count[0]).astype(jnp.float32)
    residual = live_mask * obs_weight * (sampled - innovation)
    source = picked * residual
    source_left = lax.ppermute(source, "gx", forward)
    source_right = lax.ppermute(source, "gx", backward)
    sources = jnp.concatenate([source, source_left, source_right]).reshape(1, 3 * count)

    back_block = 1024
    out = pl.pallas_call(
        functools.partial(back_kernel, back_block),
        out_shape=jax.ShapeDtypeStruct((rows, plane), jnp.float32),
        in_specs=vmem(6),
        out_specs=vmem(1)[0],
        scratch_shapes=[
            pltpu.VMEM((depth, wide), jnp.float32),
            pltpu.VMEM((padded, LANES), bf16),
            pltpu.VMEM((depth, back_block), bf16),
            pltpu.VMEM((wide, back_block), bf16),
        ],
        compiler_params=params,
        cost_estimate=pl.CostEstimate(
            flops=6 * rows * plane * count, bytes_accessed=6 * rows * plane, transcendentals=0),
        name="back",
    )(w, cells, sources, kz, ky, kx)
    return out[None]


def solution(mesh):
    return jax.shard_map(
        local,
        mesh=mesh,
        in_specs=(
            P("mem", "gx", None),
            P(None, "mem", "gx", None),
            P("gx"),
            P("gx"),
            P("gx"),
            P("gx"),
            P("gx"),
        ),
        out_specs=P("mem", "gx", None),
        check_vma=False,
    )
```

time: 384 us -> 109 us (0.28)
  the two profiles are of different devices: /device:TPU:0 before, /device:TPU:24 now
where the time goes in v1:
time: 109 us
  Pallas kernels  74.5 us (68%)
  starting transfers between devices  20.1 us (18%)
  waiting for transfers between devices  9.13 us (8%)
  other arithmetic  3.41 us (3%)
    pallas_call x1, Pallas kernels, local(): pl.pallas_call(functools.partial(sample_kernel, block), out_shape=jax.Sha...  29.5 us
    pallas_call x1, Pallas kernels, local(): pl.pallas_call(functools.partial(back_kernel, back_block), out_shape=jax....  27.2 us
    pallas_call x1, Pallas kernels, local(): pl.pallas_call(functools.partial(pick_kernel, block), out_shape=jax.Shape...  17.8 us
    ppermute x1, starting transfers between devices, local(): lax.ppermute(for_left, 'gx', backward)  4.82 us
    ppermute x1, waiting for transfers between devices, local(): cell_left = lax.ppermute(obs_cell, 'gx', forward)  4.17 us
    ppermute x1, starting transfers between devices, local(): source_left = lax.ppermute(source, 'gx', forward)  3.91 us
    ppermute x1, starting transfers between devices, local(): cell_right = lax.ppermute(obs_cell, 'gx', backward)  3.28 us
    ppermute x1, waiting for transfers between devices, local(): source_left = lax.ppermute(source, 'gx', forward)  2.6 us
  transfers between devices with their start and end apart: 9, of which 4 were waited for; matrix products, arithmetic and copies ran while one was open for 0% of the time, Pallas kernels for 16%

profile of v1, /device:TPU:24, one launch (start us, length us, event | category | flops | bytes accessed | tf_op | source)
XLA Modules:
  0.0 108.7 jit_solution(5261505100684287503)
XLA Ops:
  0.0 3.3 %collective-permute-start.1 = (s32[4096]{0:T(1024)}, s32[4096]{0:T(1024)S(1)}, u32[]{:S(2)}, u32[]{:S(2)}) collective-permute-start(s32[4096]{0:T(1024)} %param.14), channel_id=1, source_target_pairs={{1,0},{2,1},{3,2},{4,3},{5,4},{6,5},{7,6},{9,8},{10,9},{11,10},{12... | collective-permute-start | bytes 49160 | tf_op jit(solution)/shard_map/ppermute | solution.py:227
  3.3 2.6 %collective-permute-start = (s32[4096]{0:T(1024)}, s32[4096]{0:T(1024)S(1)}, u32[]{:S(2)}, u32[]{:S(2)}) collective-permute-start(s32[4096]{0:T(1024)} %param.14), channel_id=1, source_target_pairs={{0,1},{1,2},{2,3},{3,4},{4,5},{5,6},{6,7},{8,9},{9,10},{10,11},{11... | collective-permute-start | bytes 49160 | tf_op jit(solution)/shard_map/ppermute | solution.py:226
  5.8 0.0 collective-permute-done.1
  5.9 4.2 %collective-permute-done = s32[4096]{0:T(1024)S(1)} collective-permute-done((s32[4096]{0:T(1024)}, s32[4096]{0:T(1024)S(1)}, u32[]{:S(2)}, u32[]{:S(2)}) %collective-permute-start) | collective-permute-done | bytes 16416 | tf_op jit(solution)/shard_map/ppermute | solution.py:226
  10.0 1.3 %pad_add_fusion = s32[12288]{0:T(1024)} fusion(s32[4096]{0:T(1024)S(1)} %collective-permute-done.1, s32[4096]{0:T(1024)S(1)} %collective-permute-done, s32[4096]{0:T(1024)} %param.14), kind=kLoop, calls=%fused_computation | loop fusion | flops 24576 | bytes 98304 | tf_op jit(solution)/shard_map/concatenate | solution.py:230
  11.4 29.5 %sample.1 = f32[1,12288]{1,0:T(1,128)} custom-call(bf16[16,32768]{1,0:T(8,128)(2,1)} %bitcast.23, s32[1,12288]{1,0:T(1,128)} %bitcast.16, bf16[128,128]{1,0:T(8,128)(2,1)} %constant.12.clone.kz_ref, bf16[1536,256]{1,0:T(8,128)(2,1)} %constant.14.clone.kyt_ref, bf16[3,16,16]{2,1,0:T(8,128)(2,1)} %constant.15.clone.kx_ref), custom_call_target="tpu_custom_call" | custom-call | flops 12884901888 | bytes 1048576 | tf_op jit(solution)/shard_map/sample/pallas_call | solution.py:249
  40.9 0.8 fusion
  41.7 1.9 %collective-permute-start.3 = (f32[4096]{0:T(1024)S(1)}, f32[4096]{0:T(1024)S(1)}, u32[]{:S(2)}, u32[]{:S(2)}) collective-permute-start(f32[4096]{0:T(1024)S(1)} %bitcast.21), channel_id=1, source_target_pairs={{0,1},{1,2},{2,3},{3,4},{4,5},{5,6},{6,7},{8,9},{9,10},{10,11},{11... | collective-permute-start | bytes 49160 | tf_op jit(solution)/shard_map/ppermute | solution.py:265
  43.6 4.8 %collective-permute-start.2 = (f32[4096]{0:T(1024)S(1)}, f32[4096]{0:T(1024)S(1)}, u32[]{:S(2)}, u32[]{:S(2)}) collective-permute-start(f32[4096]{0:T(1024)S(1)} %bitcast.20), channel_id=1, source_target_pairs={{1,0},{2,1},{3,2},{4,3},{5,4},{6,5},{7,6},{9,8},{10,9},{11,10},{12... | collective-permute-start | bytes 49160 | tf_op jit(solution)/shard_map/ppermute | solution.py:265
  48.4 0.0 copy-start
  48.4 0.0 copy-start.1
  48.4 17.8 %pick.1 = f32[1,4096]{1,0:T(1,128)} custom-call(bf16[2,16,32768]{2,1,0:T(8,128)(2,1)} %bitcast.22, s32[1,4096]{1,0:T(1,128)} %bitcast.19, s32[1,4096]{1,0:T(1,128)} %bitcast.25, bf16[128,128]{1,0:T(8,128)(2,1)} %constant.16.clone.eye_ref), custom_call_target="tpu_custom_call" | custom-call | flops 8589934592 | bytes 2097152 | tf_op jit(solution)/shard_map/pick/pallas_call | solution.py:233
  66.2 0.0 collective-permute-done.3
  66.2 0.0 collective-permute-done.2
  66.2 0.7 add_multiply_fusion
  66.9 0.0 collective-permute-start.6
  67.0 1.6 %collective-permute-start.5 = (f32[4096]{0:T(1024)S(1)}, f32[4096]{0:T(1024)S(1)}, u32[]{:S(2)}, u32[]{:S(2)}) collective-permute-start(f32[4096]{0:T(1024)S(1)} %add_multiply_fusion), channel_id=1, source_target_pairs={{0,16},{8,24},{16,0},{24,8},{1,17},{9,25},{17,1},{25,9},{2,18},{10... | collective-permute-start | bytes 49160 | tf_op jit(solution)/shard_map/ppermute | solution.py:272
  68.5 0.2 collective-permute-start.4
  69.4 0.0 collective-permute-done.6
  69.4 1.4 %collective-permute-done.5 = f32[4096]{0:T(1024)S(1)} collective-permute-done((f32[4096]{0:T(1024)S(1)}, f32[4096]{0:T(1024)S(1)}, u32[]{:S(2)}, u32[]{:S(2)}) %collective-permute-start.5) | collective-permute-done | bytes 16416 | tf_op jit(solution)/shard_map/ppermute | solution.py:272
  70.8 0.9 collective-permute-done.4
  71.7 0.0 copy-done
  71.7 0.0 copy-done.1
  71.7 0.7 multiply_multiply_fusion
  72.4 1.9 %collective-permute-start.8 = (f32[4096]{0:T(1024)S(1)}, f32[4096]{0:T(1024)S(1)}, u32[]{:S(2)}, u32[]{:S(2)}) collective-permute-start(f32[4096]{0:T(1024)S(1)} %multiply_multiply_fusion), channel_id=1, source_target_pairs={{1,0},{2,1},{3,2},{4,3},{5,4},{6,5},{7,6},{9,8},{10,9},{11,10},{12... | collective-permute-start | bytes 49160 | tf_op jit(solution)/shard_map/ppermute | solution.py:278
  74.4 3.9 %collective-permute-start.7 = (f32[4096]{0:T(1024)S(1)}, f32[4096]{0:T(1024)S(1)}, u32[]{:S(2)}, u32[]{:S(2)}) collective-permute-start(f32[4096]{0:T(1024)S(1)} %multiply_multiply_fusion), channel_id=1, source_target_pairs={{0,1},{1,2},{2,3},{3,4},{4,5},{5,6},{6,7},{8,9},{9,10},{10,11},{11... | collective-permute-start | bytes 49160 | tf_op jit(solution)/shard_map/ppermute | solution.py:277
  78.3 0.0 collective-permute-done.8
  78.3 2.6 %collective-permute-done.7 = f32[4096]{0:T(1024)S(1)} collective-permute-done((f32[4096]{0:T(1024)S(1)}, f32[4096]{0:T(1024)S(1)}, u32[]{:S(2)}, u32[]{:S(2)}) %collective-permute-start.7) | collective-permute-done | bytes 16416 | tf_op jit(solution)/shard_map/ppermute | solution.py:277
  80.9 0.6 pad_maximum_fusion
  81.5 27.2 %back.1 = f32[16,32768]{1,0:T(8,128)} custom-call(bf16[16,32768]{1,0:T(8,128)(2,1)} %bitcast.24, s32[1,12288]{1,0:T(1,128)} %bitcast.17, f32[1,12288]{1,0:T(1,128)} %bitcast.18, bf16[128,128]{1,0:T(8,128)(2,1)} %constant.12.clone.kz_ref, bf16[256,1536]{1,0:T(8,128)(2,1)} %constant.13.clone.ky_ref, bf16[3,16,16]{2,1,0:T(8,128)(2,1)} %constant.15.clone.kx_ref), custom_call_target="tpu_custom_call" | custom-call | flops 12884901888 | bytes 3145728 | tf_op jit(solution)/shard_map/back/pallas_call | solution.py:282
Async XLA Ops:
  0.0 5.8 %collective-permute-start.1 = (s32[4096]{0:T(1024)}, s32[4096]{0:T(1024)S(1)}, u32[]{:S(2)}, u32[]{:S(2)}) collective-permute-start(s32[4096]{0:T(1024)} %param.14), channel_id=1, source_target_pairs={{1,0},{2,1},{3,2},{4,3},{5,4},{6,5},{7,6},{9,8},{10,9},{11,10},{12... | collective-permute-start | bytes 49160 | tf_op jit(solution)/shard_map/ppermute | solution.py:227
  3.3 6.7 %collective-permute-start = (s32[4096]{0:T(1024)}, s32[4096]{0:T(1024)S(1)}, u32[]{:S(2)}, u32[]{:S(2)}) collective-permute-start(s32[4096]{0:T(1024)} %param.14), channel_id=1, source_target_pairs={{0,1},{1,2},{2,3},{3,4},{4,5},{5,6},{6,7},{8,9},{9,10},{10,11},{11... | collective-permute-start | bytes 49160 | tf_op jit(solution)/shard_map/ppermute | solution.py:226
  41.7 24.6 %collective-permute-start.3 = (f32[4096]{0:T(1024)S(1)}, f32[4096]{0:T(1024)S(1)}, u32[]{:S(2)}, u32[]{:S(2)}) collective-permute-start(f32[4096]{0:T(1024)S(1)} %bitcast.21), channel_id=1, source_target_pairs={{0,1},{1,2},{2,3},{3,4},{4,5},{5,6},{6,7},{8,9},{9,10},{10,11},{11... | collective-permute-start | bytes 49160 | tf_op jit(solution)/shard_map/ppermute | solution.py:265
  43.6 22.6 %collective-permute-start.2 = (f32[4096]{0:T(1024)S(1)}, f32[4096]{0:T(1024)S(1)}, u32[]{:S(2)}, u32[]{:S(2)}) collective-permute-start(f32[4096]{0:T(1024)S(1)} %bitcast.20), channel_id=1, source_target_pairs={{1,0},{2,1},{3,2},{4,3},{5,4},{6,5},{7,6},{9,8},{10,9},{11,10},{12... | collective-permute-start | bytes 49160 | tf_op jit(solution)/shard_map/ppermute | solution.py:265
  48.4 23.3 %copy-start = (f32[4096]{0:T(1024)S(1)}, f32[4096]{0:T(1024)}, u32[]{:S(2)}) copy-start(f32[4096]{0:T(1024)} %param.16) | copy-start | bytes 49156
  48.4 23.3 %copy-start.1 = (f32[4096]{0:T(1024)S(1)}, f32[4096]{0:T(1024)}, u32[]{:S(2)}) copy-start(f32[4096]{0:T(1024)} %param.17) | copy-start | bytes 49156
  66.9 2.4 %collective-permute-start.6 = (f32[4096]{0:T(1024)S(1)}, f32[4096]{0:T(1024)S(1)}, u32[]{:S(2)}, u32[]{:S(2)}) collective-permute-start(f32[4096]{0:T(1024)S(1)} %add_multiply_fusion), channel_id=1, source_target_pairs={{0,24},{8,0},{16,8},{24,16},{1,25},{9,1},{17,9},{25,17},{2,26},{10... | collective-permute-start | bytes 49160 | tf_op jit(solution)/shard_map/ppermute | solution.py:272
  67.0 3.8 %collective-permute-start.5 = (f32[4096]{0:T(1024)S(1)}, f32[4096]{0:T(1024)S(1)}, u32[]{:S(2)}, u32[]{:S(2)}) collective-permute-start(f32[4096]{0:T(1024)S(1)} %add_multiply_fusion), channel_id=1, source_target_pairs={{0,16},{8,24},{16,0},{24,8},{1,17},{9,25},{17,1},{25,9},{2,18},{10... | collective-permute-start | bytes 49160 | tf_op jit(solution)/shard_map/ppermute | solution.py:272
  68.5 3.2 %collective-permute-start.4 = (f32[4096]{0:T(1024)S(1)}, f32[4096]{0:T(1024)S(1)}, u32[]{:S(2)}, u32[]{:S(2)}) collective-permute-start(f32[4096]{0:T(1024)S(1)} %add_multiply_fusion), channel_id=1, source_target_pairs={{0,8},{8,16},{16,24},{24,0},{1,9},{9,17},{17,25},{25,1},{2,10},{10... | collective-permute-start | bytes 49160 | tf_op jit(solution)/shard_map/ppermute | solution.py:272
  72.4 5.9 %collective-permute-start.8 = (f32[4096]{0:T(1024)S(1)}, f32[4096]{0:T(1024)S(1)}, u32[]{:S(2)}, u32[]{:S(2)}) collective-permute-start(f32[4096]{0:T(1024)S(1)} %multiply_multiply_fusion), channel_id=1, source_target_pairs={{1,0},{2,1},{3,2},{4,3},{5,4},{6,5},{7,6},{9,8},{10,9},{11,10},{12... | collective-permute-start | bytes 49160 | tf_op jit(solution)/shard_map/ppermute | solution.py:278
  74.4 6.5 %collective-permute-start.7 = (f32[4096]{0:T(1024)S(1)}, f32[4096]{0:T(1024)S(1)}, u32[]{:S(2)}, u32[]{:S(2)}) collective-permute-start(f32[4096]{0:T(1024)S(1)} %multiply_multiply_fusion), channel_id=1, source_target_pairs={{0,1},{1,2},{2,3},{3,4},{4,5},{5,6},{6,7},{8,9},{9,10},{10,11},{11... | collective-permute-start | bytes 49160 | tf_op jit(solution)/shard_map/ppermute | solution.py:277

commit v2 on v1

--- a/solution.py
+++ b/solution.py
@@ -19,6 +19,7 @@
 HIGH = PAIRS // LOW
 VMEM_LIMIT = 56 * 1024 * 1024
 NT = (((1,), (1,)), ((), ()))
+MESH = pl.DeviceIdType.MESH
 
 
 def tap_values():
@@ -197,6 +198,108 @@
             out_ref[:, lane] = z[j * rows:(j + 1) * rows] + w_ref[:, lane].astype(jnp.float32)
 
 
+def greet(neighbours):
+    barrier = pltpu.get_barrier_semaphore()
+    expected = 0
+    for there, where in neighbours:
+        if there is True:
+            pl.semaphore_signal(barrier, inc=1, device_id=where, device_id_type=MESH)
+            expected = expected + 1
+        else:
+            @pl.when(there)
+            def _():
+                pl.semaphore_signal(barrier, inc=1, device_id=where, device_id_type=MESH)
+            expected = expected + there.astype(jnp.int32)
+    pl.semaphore_wait(barrier, expected)
+
+
+def slab_sides():
+    me = lax.axis_index("gx")
+    return (me > 0, {"gx": me - 1}), (me < lax.axis_size("gx") - 1, {"gx": me + 1})
+
+
+def both_ways(to_left, to_right, from_left, from_right, send, recv):
+    (has_left, left), (has_right, right) = slab_sides()
+    leftward = pltpu.make_async_remote_copy(
+        src_ref=to_left, dst_ref=from_right, send_sem=send.at[0], recv_sem=recv.at[0],
+        device_id=left, device_id_type=MESH)
+    rightward = pltpu.make_async_remote_copy(
+        src_ref=to_right, dst_ref=from_left, send_sem=send.at[1], recv_sem=recv.at[1],
+        device_id=right, device_id_type=MESH)
+    pl.when(has_left)(leftward.start)
+    pl.when(has_right)(rightward.start)
+
+    def arrived():
+        pl.when(has_left)(rightward.wait_recv)
+        pl.when(has_right)(leftward.wait_recv)
+
+        @pl.when(jnp.logical_not(has_left))
+        def _():
+            from_left[...] = jnp.zeros_like(from_left)
+
+        @pl.when(jnp.logical_not(has_right))
+        def _():
+            from_right[...] = jnp.zeros_like(from_right)
+
+    def sent():
+        pl.when(has_left)(leftward.wait_send)
+        pl.when(has_right)(rightward.wait_send)
+
+    return arrived, sent
+
+
+def cells_kernel(cell_ref, out_ref, left_ref, right_ref, send, recv):
+    count = cell_ref.shape[1]
+    greet(slab_sides())
+    arrived, sent = both_ways(cell_ref, cell_ref, left_ref, right_ref, send, recv)
+    out_ref[:, :count] = cell_ref[...]
+    arrived()
+    out_ref[:, count:2 * count] = left_ref[...]
+    out_ref[:, 2 * count:] = right_ref[...]
+    sent()
+
+
+def residual_kernel(s_ref, pick_ref, innovation_ref, weight_ref, count_ref, out_ref,
+                    to_left, to_right, s_left, s_right, share, peers, source, v_left, v_right,
+                    s_send, s_recv, m_send, m_recv, v_send, v_recv):
+    count = pick_ref.shape[1]
+    members = lax.axis_size("mem")
+    here = lax.axis_index("mem")
+    others = [(True, {"mem": lax.rem(here + step, members)}) for step in range(1, members)]
+    greet(list(slab_sides()) + others)
+
+    to_left[...] = s_ref[:, count:2 * count]
+    to_right[...] = s_ref[:, 2 * count:]
+    arrived, s_sent = both_ways(to_left, to_right, s_left, s_right, s_send, s_recv)
+    arrived()
+    own = s_ref[:, :count] + s_left[...] + s_right[...]
+    share[...] = pick_ref[...] * own
+
+    copies = []
+    for k, (_, where) in enumerate(others):
+        copies.append(pltpu.make_async_remote_copy(
+            src_ref=share, dst_ref=peers.at[k], send_sem=m_send.at[k], recv_sem=m_recv.at[k],
+            device_id=where, device_id_type=MESH))
+        copies[-1].start()
+    sampled = share[...]
+    for k, copy in enumerate(copies):
+        copy.wait_recv()
+        sampled = sampled + peers[k]
+    live = lax.broadcasted_iota(jnp.int32, (1, count), 1) < count_ref[0]
+    residual = jnp.where(live, weight_ref[...], 0.0) * (sampled - innovation_ref[...])
+    source[...] = pick_ref[...] * residual
+
+    arrived, v_sent = both_ways(source, source, v_left, v_right, v_send, v_recv)
+    out_ref[:, :count] = source[...]
+    arrived()
+    out_ref[:, count:2 * count] = v_left[...]
+    out_ref[:, 2 * count:] = v_right[...]
+    s_sent()
+    for copy in copies:
+        copy.wait_send()
+    v_sent()
+
+
 def vmem(count):
     return [pl.BlockSpec(memory_space=pltpu.VMEM)] * count
 
@@ -213,23 +316,25 @@
     params = pltpu.CompilerParams(vmem_limit_bytes=VMEM_LIMIT)
     bf16 = jnp.bfloat16
 
-    slabs = lax.axis_size("gx")
-    forward = [(i, i + 1) for i in range(slabs - 1)]
-    backward = [(b, a) for a, b in forward]
-
     kz = jnp.asarray(z_band())
     ky_np = y_band(rows)
     ky, kyt = jnp.asarray(ky_np), jnp.asarray(np.ascontiguousarray(ky_np.T))
     kx = jnp.asarray(x_bands(rows))
     eye = jnp.asarray(np.eye(LANES).astype(ml_dtypes.bfloat16))
 
-    cell_left = lax.ppermute(obs_cell, "gx", forward)
-    cell_right = lax.ppermute(obs_cell, "gx", backward)
     cell = obs_cell.reshape(1, count)
     slot = obs_slot.reshape(1, count)
-    cells = jnp.concatenate([obs_cell, cell_left, cell_right]).reshape(1, 3 * count)
-
-    block = 512
+    cells = pl.pallas_call(
+        cells_kernel,
+        out_shape=jax.ShapeDtypeStruct((1, 3 * count), jnp.int32),
+        in_specs=vmem(1),
+        out_specs=vmem(1)[0],
+        scratch_shapes=[pltpu.VMEM((1, count), jnp.int32)] * 2 + [pltpu.SemaphoreType.DMA((2,))] * 2,
+        compiler_params=pltpu.CompilerParams(collective_id=0, has_side_effects=True),
+        name="cells",
+    )(cell)
+
+    block = 2048
     picked = pl.pallas_call(
         functools.partial(pick_kernel, block),
         out_shape=jax.ShapeDtypeStruct((1, count), jnp.float32),
@@ -260,25 +365,24 @@
         cost_estimate=pl.CostEstimate(
             flops=6 * rows * plane * count, bytes_accessed=2 * rows * plane, transcendentals=0),
         name="sample",
-    )(w, cells, kz, kyt, kx)[0]
-    own, for_left, for_right = sampled3[:count], sampled3[count:2 * count], sampled3[2 * count:]
-    own = own + lax.ppermute(for_left, "gx", backward) + lax.ppermute(for_right, "gx", forward)
-
-    picked = picked[0]
-    share = picked * own
-    members = lax.axis_size("mem")
-    sampled = share
-    for step in range(1, members):
-        sampled = sampled + lax.ppermute(
-            share, "mem", [(i, (i + step) % members) for i in range(members)])
-    live_mask = (jnp.arange(count) < obs_count[0]).astype(jnp.float32)
-    residual = live_mask * obs_weight * (sampled - innovation)
-    source = picked * residual
-    source_left = lax.ppermute(source, "gx", forward)
-    source_right = lax.ppermute(source, "gx", backward)
-    sources = jnp.concatenate([source, source_left, source_right]).reshape(1, 3 * count)
-
-    back_block = 1024
+    )(w, cells, kz, kyt, kx)
+
+    peers = lax.axis_size("mem") - 1
+    line = pltpu.VMEM((1, count), jnp.float32)
+    pair = pltpu.SemaphoreType.DMA((2,))
+    each = pltpu.SemaphoreType.DMA((peers,))
+    sources = pl.pallas_call(
+        residual_kernel,
+        out_shape=jax.ShapeDtypeStruct((1, 3 * count), jnp.float32),
+        in_specs=vmem(4) + [pl.BlockSpec(memory_space=pltpu.SMEM)],
+        out_specs=vmem(1)[0],
+        scratch_shapes=[line] * 5 + [pltpu.VMEM((peers, 1, count), jnp.float32)] + [line] * 3
+        + [pair, pair, each, each, pair, pair],
+        compiler_params=pltpu.CompilerParams(collective_id=1, has_side_effects=True),
+        name="residual",
+    )(sampled3, picked, innovation.reshape(1, count), obs_weight.reshape(1, count), obs_count)
+
+    back_block = 2048
     out = pl.pallas_call(
         functools.partial(back_kernel, back_block),
         out_shape=jax.ShapeDtypeStruct((rows, plane), jnp.float32),

time: 109 us -> 88.1 us (0.81)
  the two profiles are of different devices: /device:TPU:24 before, /device:TPU:0 now
where the time goes in v2:
time: 88.1 us; the launch traced here: 87.7 us
  Pallas kernels  87 us (99%)
    pallas_call x1, Pallas kernels, local(): pl.pallas_call(functools.partial(back_kernel, back_block), out_shape=jax....  25.6 us
    pallas_call x1, Pallas kernels, local(): pl.pallas_call(functools.partial(sample_kernel, block), out_shape=jax.Sha...  24.4 us
    pallas_call x1, Pallas kernels, local(): pl.pallas_call(functools.partial(pick_kernel, block), out_shape=jax.Shape...  16.7 us
    pallas_call x1, Pallas kernels, local(): pl.pallas_call(residual_kernel, out_shape=jax.ShapeDtypeStruct((1, 3 * co...  12.8 us
    pallas_call x1, Pallas kernels, local(): pl.pallas_call(cells_kernel, out_shape=jax.ShapeDtypeStruct((1, 3 * count...  7.57 us

profile of v2, /device:TPU:0, one launch (start us, length us, event | category | flops | bytes accessed | tf_op | source)
XLA Modules:
  0.0 87.7 jit_solution(4149816195792039553)
XLA Ops:
  0.7 16.7 %pick.1.pick_ref = f32[1,4096]{1,0:T(1,128)} custom-call(bf16[2,16,32768]{2,1,0:T(8,128)(2,1)} %bitcast.11, s32[1,4096]{1,0:T(1,128)} %bitcast.9, s32[1,4096]{1,0:T(1,128)} %bitcast.14, bf16[128,128]{1,0:T(8,128)(2,1)} %constant.14.clone.eye_ref), custom_call_target="tpu_custom_call" | custom-call | flops 8589934592 | bytes 2097152 | tf_op jit(solution)/shard_map/pick/pallas_call | solution.py:338
  17.4 7.6 %cells.1.cell_ref = s32[1,12288]{1,0:T(1,128)} custom-call(s32[1,4096]{1,0:T(1,128)} %bitcast.10), custom_call_target="tpu_custom_call" | custom-call | tf_op jit(solution)/shard_map/cells/pallas_call | solution.py:327
  24.9 24.4 %sample.1.s_ref = f32[1,12288]{1,0:T(1,128)} custom-call(bf16[16,32768]{1,0:T(8,128)(2,1)} %bitcast.12, s32[1,12288]{1,0:T(1,128)} %cells.1.cell_ref, bf16[128,128]{1,0:T(8,128)(2,1)} %constant.10.clone.kz_ref, bf16[1536,256]{1,0:T(8,128)(2,1)} %constant.12.clone.kyt_ref, bf16[3,16,16]{2,1,0:T(8,128)(2,1)} %constant.13.clone.kx_ref), custom_call_target="tpu_custom_call" | custom-call | flops 12884901888 | bytes 1048576 | tf_op jit(solution)/shard_map/sample/pallas_call | solution.py:354
  49.3 12.8 %residual.1.v_ref = f32[1,12288]{1,0:T(1,128)} custom-call(f32[1,12288]{1,0:T(1,128)} %sample.1.s_ref, f32[1,4096]{1,0:T(1,128)} %pick.1.pick_ref, f32[1,4096]{1,0:T(1,128)} %bitcast.7, f32[1,4096]{1,0:T(1,128)} %bitcast.8, s32[1]{0:T(128)S(6)} %copy.13.count_ref), custom_call_target="tpu_custom_call" | custom-call | tf_op jit(solution)/shard_map/residual/pallas_call | solution.py:374
  62.1 25.6 %back.1 = f32[16,32768]{1,0:T(8,128)} custom-call(bf16[16,32768]{1,0:T(8,128)(2,1)} %bitcast.13, s32[1,12288]{1,0:T(1,128)} %cells.1.cell_ref, f32[1,12288]{1,0:T(1,128)} %residual.1.v_ref, bf16[128,128]{1,0:T(8,128)(2,1)} %constant.10.clone.kz_ref, bf16[256,1536]{1,0:T(8,128)(2,1)} %constant.11.clone.ky_ref, bf16[3,16,16]{2,1,0:T(8,128)(2,1)} %constant.13.clone.kx_ref), custom_call_target="tpu_custom_call" | custom-call | flops 12884901888 | bytes 3145728 | tf_op jit(solution)/shard_map/back/pallas_call | solution.py:386

commit v3 on v2

--- a/solution.py
+++ b/solution.py
@@ -17,6 +17,8 @@
 PAIRS = NY // 2
 LOW = 64
 HIGH = PAIRS // LOW
+UNROLL = 2
+SUB = 512
 VMEM_LIMIT = 56 * 1024 * 1024
 NT = (((1,), (1,)), ((), ()))
 MESH = pl.DeviceIdType.MESH
@@ -82,6 +84,17 @@
     return jnp.dot(kx, hot, preferred_element_type=jnp.float32).astype(jnp.bfloat16)
 
 
+def looked_up(table_ref, a_ref, x_rows, low, row, rows):
+    found = []
+    for j in range(0, x_rows.shape[1], SUB):
+        part = slice(j, j + SUB)
+        fill_a(a_ref.at[:, part], x_rows[:, part], low[:, part], rows)
+        m = jnp.dot(table_ref[...], a_ref[:, part], preferred_element_type=jnp.float32)
+        hit = lax.broadcasted_iota(jnp.int32, m.shape, 0) == row[:, part]
+        found.append(jnp.sum(jnp.where(hit, m, 0.0), axis=0, keepdims=True))
+    return jnp.concatenate(found, axis=1)
+
+
 def pairs_block(w_ref, b, rows):
     parts = []
     for j in range(16):
@@ -98,13 +111,13 @@
     z_ref[:, :pad] = jnp.zeros((LANES, pad), jnp.bfloat16)
     z_ref[:, pad + PAIRS * rows:] = jnp.zeros((LANES, pad), jnp.bfloat16)
 
-    @pl.loop(0, PAIRS // 16)
+    @pl.loop(0, PAIRS // 16, unroll=UNROLL)
     def _(b):
         part = pairs_block(w_ref, b, rows)
         z = lax.dot_general(kz_ref[...], part, NT, preferred_element_type=jnp.float32)
         z_ref[:, pl.ds(pl.multiple_of(pad + b * span, LANES), span)] = z.astype(jnp.bfloat16)
 
-    @pl.loop(0, PAIRS // 16)
+    @pl.loop(0, PAIRS // 16, unroll=UNROLL)
     def _(b):
         win = z_ref[:, pl.ds(pl.multiple_of(b * span, LANES), 2 * span)]
         top, bottom = win[:NZ], win[NZ:]
@@ -125,10 +138,7 @@
         at = pl.ds(pl.multiple_of(i * block, block), block)
         x, low, row = split_cell(cell_ref[:, at])
         kx = kx_ref[i // (per_list // block)]
-        fill_a(a_ref, x_taps(kx, x, rows), low, rows)
-        m = jnp.dot(y_ref[...], a_ref[...], preferred_element_type=jnp.float32)
-        hit = lax.broadcasted_iota(jnp.int32, m.shape, 0) == row
-        s_ref[:, at] = jnp.sum(jnp.where(hit, m, 0.0), axis=0, keepdims=True)
+        s_ref[:, at] = looked_up(y_ref, a_ref, x_taps(kx, x, rows), low, row, rows)
 
 
 def pick_kernel(block, p_ref, cell_ref, slot_ref, eye_ref, o_ref, t_ref, a_ref):
@@ -136,7 +146,7 @@
     span = 16 * rows
 
     for t in range(slots):
-        @pl.loop(0, PAIRS // 16)
+        @pl.loop(0, PAIRS // 16, unroll=UNROLL)
         def _(b):
             part = pairs_block(p_ref.at[t], b, rows)
             z = lax.dot_general(eye_ref[...], part, NT, preferred_element_type=jnp.float32)
@@ -150,10 +160,7 @@
         at = pl.ds(pl.multiple_of(i * block, block), block)
         x, low, row = split_cell(cell_ref[:, at])
         row = row + slot_ref[:, at] * (HIGH * LANES)
-        fill_a(a_ref, x_taps(None, x, rows), low, rows)
-        m = jnp.dot(t_ref[...], a_ref[...], preferred_element_type=jnp.float32)
-        hit = lax.broadcasted_iota(jnp.int32, m.shape, 0) == row
-        o_ref[:, at] = jnp.sum(jnp.where(hit, m, 0.0), axis=0, keepdims=True)
+        o_ref[:, at] = looked_up(t_ref, a_ref, x_taps(None, x, rows), low, row, rows)
 
 
 def back_kernel(block, w_ref, cell_ref, v_ref, kz_ref, ky_ref, kx_ref, out_ref,
@@ -183,7 +190,7 @@
         x_ref[pad + h * depth:pad + (h + 1) * depth, :] = g_ref[
             :, h * LANES:(h + 1) * LANES].astype(jnp.bfloat16)
 
-    @pl.loop(0, PAIRS // 16)
+    @pl.loop(0, PAIRS // 16, unroll=UNROLL)
     def _(b):
         win = x_ref[pl.ds(pl.multiple_of(b * span, LANES), 2 * span), :]
         first, second = win[:, :NZ], win[:, NZ:]

time: 88.1 us -> 82.2 us (0.933)
  Pallas kernels: 87 us -> 81.2 us
    pallas_call x1, Pallas kernels: 24.4 us -> 21.9 us  [local(): pl.pallas_call(functools.partial(sample_kernel, block), out_shape=jax.Sha...]
    pallas_call x1, Pallas kernels: 16.7 us -> 14.6 us  [local(): pl.pallas_call(functools.partial(pick_kernel, block), out_shape=jax.Shape...]
    pallas_call x1, Pallas kernels: 25.6 us -> 24.4 us  [local(): pl.pallas_call(functools.partial(back_kernel, back_block), out_shape=jax....]
where the time goes in v3:
time: 82.2 us; the launch traced here: 81.9 us
  Pallas kernels  81.2 us (99%)
    pallas_call x1, Pallas kernels, local(): pl.pallas_call(functools.partial(back_kernel, back_block), out_shape=jax....  24.4 us
    pallas_call x1, Pallas kernels, local(): pl.pallas_call(functools.partial(sample_kernel, block), out_shape=jax.Sha...  21.9 us
    pallas_call x1, Pallas kernels, local(): pl.pallas_call(functools.partial(pick_kernel, block), out_shape=jax.Shape...  14.6 us
    pallas_call x1, Pallas kernels, local(): pl.pallas_call(residual_kernel, out_shape=jax.ShapeDtypeStruct((1, 3 * co...  12.8 us
    pallas_call x1, Pallas kernels, local(): pl.pallas_call(cells_kernel, out_shape=jax.ShapeDtypeStruct((1, 3 * count...  7.57 us

profile of v3, /device:TPU:0, one launch (start us, length us, event | category | flops | bytes accessed | tf_op | source)
XLA Modules:
  0.0 81.9 jit_solution(297737843295210714)
XLA Ops:
  0.7 14.6 %pick.1.pick_ref = f32[1,4096]{1,0:T(1,128)} custom-call(bf16[2,16,32768]{2,1,0:T(8,128)(2,1)} %bitcast.11, s32[1,4096]{1,0:T(1,128)} %bitcast.9, s32[1,4096]{1,0:T(1,128)} %bitcast.14, bf16[128,128]{1,0:T(8,128)(2,1)} %constant.14.clone.eye_ref), custom_call_target="tpu_custom_call" | custom-call | flops 8589934592 | bytes 2097152 | tf_op jit(solution)/shard_map/pick/pallas_call | solution.py:345
  15.2 7.6 %cells.1.cell_ref = s32[1,12288]{1,0:T(1,128)} custom-call(s32[1,4096]{1,0:T(1,128)} %bitcast.10), custom_call_target="tpu_custom_call" | custom-call | tf_op jit(solution)/shard_map/cells/pallas_call | solution.py:334
  22.8 21.9 %sample.1.s_ref = f32[1,12288]{1,0:T(1,128)} custom-call(bf16[16,32768]{1,0:T(8,128)(2,1)} %bitcast.12, s32[1,12288]{1,0:T(1,128)} %cells.1.cell_ref, bf16[128,128]{1,0:T(8,128)(2,1)} %constant.10.clone.kz_ref, bf16[1536,256]{1,0:T(8,128)(2,1)} %constant.12.clone.kyt_ref, bf16[3,16,16]{2,1,0:T(8,128)(2,1)} %constant.13.clone.kx_ref), custom_call_target="tpu_custom_call" | custom-call | flops 12884901888 | bytes 1048576 | tf_op jit(solution)/shard_map/sample/pallas_call | solution.py:361
  44.7 12.8 %residual.1.v_ref = f32[1,12288]{1,0:T(1,128)} custom-call(f32[1,12288]{1,0:T(1,128)} %sample.1.s_ref, f32[1,4096]{1,0:T(1,128)} %pick.1.pick_ref, f32[1,4096]{1,0:T(1,128)} %bitcast.7, f32[1,4096]{1,0:T(1,128)} %bitcast.8, s32[1]{0:T(128)S(6)} %copy.13.count_ref), custom_call_target="tpu_custom_call" | custom-call | tf_op jit(solution)/shard_map/residual/pallas_call | solution.py:381
  57.5 24.4 %back.1 = f32[16,32768]{1,0:T(8,128)} custom-call(bf16[16,32768]{1,0:T(8,128)(2,1)} %bitcast.13, s32[1,12288]{1,0:T(1,128)} %cells.1.cell_ref, f32[1,12288]{1,0:T(1,128)} %residual.1.v_ref, bf16[128,128]{1,0:T(8,128)(2,1)} %constant.10.clone.kz_ref, bf16[256,1536]{1,0:T(8,128)(2,1)} %constant.11.clone.ky_ref, bf16[3,16,16]{2,1,0:T(8,128)(2,1)} %constant.13.clone.kx_ref), custom_call_target="tpu_custom_call" | custom-call | flops 12884901888 | bytes 3145728 | tf_op jit(solution)/shard_map/back/pallas_call | solution.py:393

commit v4 on v3

--- a/solution.py
+++ b/solution.py
@@ -17,8 +17,9 @@
 PAIRS = NY // 2
 LOW = 64
 HIGH = PAIRS // LOW
-UNROLL = 2
+UNROLL = 4
 SUB = 512
+BACK_SUB = 1024
 VMEM_LIMIT = 56 * 1024 * 1024
 NT = (((1,), (1,)), ((), ()))
 MESH = pl.DeviceIdType.MESH
@@ -177,12 +178,16 @@
         at = pl.ds(pl.multiple_of(i * block, block), block)
         x, low, row = split_cell(cell_ref[:, at])
         kx = kx_ref[i // (per_list // block)]
-        fill_a(a_ref, x_taps(kx, x, rows), low, rows)
-        shape = (HIGH * LANES, block)
-        hit = lax.broadcasted_iota(jnp.int32, shape, 0) == row
-        b_ref[...] = jnp.where(hit, v_ref[:, at], 0.0).astype(jnp.bfloat16)
-        g_ref[...] += lax.dot_general(
-            a_ref[...], b_ref[...], NT, preferred_element_type=jnp.float32)
+        x_rows, value = x_taps(kx, x, rows), v_ref[:, at]
+        total = g_ref[...]
+        for j in range(0, block, BACK_SUB):
+            part = slice(j, j + BACK_SUB)
+            fill_a(a_ref.at[:, part], x_rows[:, part], low[:, part], rows)
+            hit = lax.broadcasted_iota(jnp.int32, (HIGH * LANES, BACK_SUB), 0) == row[:, part]
+            b_ref[:, part] = jnp.where(hit, value[:, part], 0.0).astype(jnp.bfloat16)
+            total = total + lax.dot_general(
+                a_ref[:, part], b_ref[:, part], NT, preferred_element_type=jnp.float32)
+        g_ref[...] = total
 
     x_ref[:pad, :] = jnp.zeros((pad, LANES), jnp.bfloat16)
     x_ref[pad + PAIRS * rows:, :] = jnp.zeros((pad, LANES), jnp.bfloat16)

time: 82.2 us -> 78.8 us (0.959)
  Pallas kernels: 81.2 us -> 77.8 us
    pallas_call x1, Pallas kernels: 21.9 us -> 20.5 us  [local(): pl.pallas_call(functools.partial(sample_kernel, block), out_shape=jax.Sha...]
    pallas_call x1, Pallas kernels: 14.6 us -> 13.3 us  [local(): pl.pallas_call(functools.partial(pick_kernel, block), out_shape=jax.Shape...]
where the time goes in v4:
time: 78.8 us; the launch traced here: 78.5 us
  Pallas kernels  77.8 us (99%)
    pallas_call x1, Pallas kernels, local(): pl.pallas_call(functools.partial(back_kernel, back_block), out_shape=jax....  23.6 us
    pallas_call x1, Pallas kernels, local(): pl.pallas_call(functools.partial(sample_kernel, block), out_shape=jax.Sha...  20.5 us
    pallas_call x1, Pallas kernels, local(): pl.pallas_call(functools.partial(pick_kernel, block), out_shape=jax.Shape...  13.3 us
    pallas_call x1, Pallas kernels, local(): pl.pallas_call(residual_kernel, out_shape=jax.ShapeDtypeStruct((1, 3 * co...  12.8 us
    pallas_call x1, Pallas kernels, local(): pl.pallas_call(cells_kernel, out_shape=jax.ShapeDtypeStruct((1, 3 * count...  7.58 us

profile of v4, /device:TPU:0, one launch (start us, length us, event | category | flops | bytes accessed | tf_op | source)
XLA Modules:
  0.0 78.5 jit_solution(16017078369937281695)
XLA Ops:
  0.7 13.3 %pick.1.pick_ref = f32[1,4096]{1,0:T(1,128)} custom-call(bf16[2,16,32768]{2,1,0:T(8,128)(2,1)} %bitcast.11, s32[1,4096]{1,0:T(1,128)} %bitcast.9, s32[1,4096]{1,0:T(1,128)} %bitcast.14, bf16[128,128]{1,0:T(8,128)(2,1)} %constant.14.clone.eye_ref), custom_call_target="tpu_custom_call" | custom-call | flops 8589934592 | bytes 2097152 | tf_op jit(solution)/shard_map/pick/pallas_call | solution.py:350
  14.0 7.6 %cells.1.cell_ref = s32[1,12288]{1,0:T(1,128)} custom-call(s32[1,4096]{1,0:T(1,128)} %bitcast.10), custom_call_target="tpu_custom_call" | custom-call | tf_op jit(solution)/shard_map/cells/pallas_call | solution.py:339
  21.5 20.5 %sample.1.s_ref = f32[1,12288]{1,0:T(1,128)} custom-call(bf16[16,32768]{1,0:T(8,128)(2,1)} %bitcast.12, s32[1,12288]{1,0:T(1,128)} %cells.1.cell_ref, bf16[128,128]{1,0:T(8,128)(2,1)} %constant.10.clone.kz_ref, bf16[1536,256]{1,0:T(8,128)(2,1)} %constant.12.clone.kyt_ref, bf16[3,16,16]{2,1,0:T(8,128)(2,1)} %constant.13.clone.kx_ref), custom_call_target="tpu_custom_call" | custom-call | flops 12884901888 | bytes 1048576 | tf_op jit(solution)/shard_map/sample/pallas_call | solution.py:366
  42.1 12.8 %residual.1.v_ref = f32[1,12288]{1,0:T(1,128)} custom-call(f32[1,12288]{1,0:T(1,128)} %sample.1.s_ref, f32[1,4096]{1,0:T(1,128)} %pick.1.pick_ref, f32[1,4096]{1,0:T(1,128)} %bitcast.7, f32[1,4096]{1,0:T(1,128)} %bitcast.8, s32[1]{0:T(128)S(6)} %copy.13.count_ref), custom_call_target="tpu_custom_call" | custom-call | tf_op jit(solution)/shard_map/residual/pallas_call | solution.py:386
  54.9 23.6 %back.1 = f32[16,32768]{1,0:T(8,128)} custom-call(bf16[16,32768]{1,0:T(8,128)(2,1)} %bitcast.13, s32[1,12288]{1,0:T(1,128)} %cells.1.cell_ref, f32[1,12288]{1,0:T(1,128)} %residual.1.v_ref, bf16[128,128]{1,0:T(8,128)(2,1)} %constant.10.clone.kz_ref, bf16[256,1536]{1,0:T(8,128)(2,1)} %constant.11.clone.ky_ref, bf16[3,16,16]{2,1,0:T(8,128)(2,1)} %constant.13.clone.kx_ref), custom_call_target="tpu_custom_call" | custom-call | flops 12884901888 | bytes 3145728 | tf_op jit(solution)/shard_map/back/pallas_call | solution.py:398

commit v5 on v4

--- a/solution.py
+++ b/solution.py
@@ -17,7 +17,7 @@
 PAIRS = NY // 2
 LOW = 64
 HIGH = PAIRS // LOW
-UNROLL = 4
+UNROLL = 8
 SUB = 512
 BACK_SUB = 1024
 VMEM_LIMIT = 56 * 1024 * 1024

time: 78.8 us -> 77.3 us (0.981)
  Pallas kernels: 77.8 us -> 76.3 us
where the time goes in v5:
time: 77.3 us; the launch traced here: 77 us
  Pallas kernels  76.3 us (99%)
    pallas_call x1, Pallas kernels, local(): pl.pallas_call(functools.partial(back_kernel, back_block), out_shape=jax....  23.3 us
    pallas_call x1, Pallas kernels, local(): pl.pallas_call(functools.partial(sample_kernel, block), out_shape=jax.Sha...  19.9 us
    pallas_call x1, Pallas kernels, local(): pl.pallas_call(functools.partial(pick_kernel, block), out_shape=jax.Shape...  12.8 us
    pallas_call x1, Pallas kernels, local(): pl.pallas_call(residual_kernel, out_shape=jax.ShapeDtypeStruct((1, 3 * co...  12.8 us
    pallas_call x1, Pallas kernels, local(): pl.pallas_call(cells_kernel, out_shape=jax.ShapeDtypeStruct((1, 3 * count...  7.57 us

profile of v5, /device:TPU:0, one launch (start us, length us, event | category | flops | bytes accessed | tf_op | source)
XLA Modules:
  0.0 77.0 jit_solution(5449954271771813411)
XLA Ops:
  0.7 12.8 %pick.1.pick_ref = f32[1,4096]{1,0:T(1,128)} custom-call(bf16[2,16,32768]{2,1,0:T(8,128)(2,1)} %bitcast.11, s32[1,4096]{1,0:T(1,128)} %bitcast.9, s32[1,4096]{1,0:T(1,128)} %bitcast.14, bf16[128,128]{1,0:T(8,128)(2,1)} %constant.14.clone.eye_ref), custom_call_target="tpu_custom_call" | custom-call | flops 8589934592 | bytes 2097152 | tf_op jit(solution)/shard_map/pick/pallas_call | solution.py:350
  13.5 7.6 %cells.1.cell_ref = s32[1,12288]{1,0:T(1,128)} custom-call(s32[1,4096]{1,0:T(1,128)} %bitcast.10), custom_call_target="tpu_custom_call" | custom-call | tf_op jit(solution)/shard_map/cells/pallas_call | solution.py:339
  21.1 19.9 %sample.1.s_ref = f32[1,12288]{1,0:T(1,128)} custom-call(bf16[16,32768]{1,0:T(8,128)(2,1)} %bitcast.12, s32[1,12288]{1,0:T(1,128)} %cells.1.cell_ref, bf16[128,128]{1,0:T(8,128)(2,1)} %constant.10.clone.kz_ref, bf16[1536,256]{1,0:T(8,128)(2,1)} %constant.12.clone.kyt_ref, bf16[3,16,16]{2,1,0:T(8,128)(2,1)} %constant.13.clone.kx_ref), custom_call_target="tpu_custom_call" | custom-call | flops 12884901888 | bytes 1048576 | tf_op jit(solution)/shard_map/sample/pallas_call | solution.py:366
  40.9 12.8 %residual.1.v_ref = f32[1,12288]{1,0:T(1,128)} custom-call(f32[1,12288]{1,0:T(1,128)} %sample.1.s_ref, f32[1,4096]{1,0:T(1,128)} %pick.1.pick_ref, f32[1,4096]{1,0:T(1,128)} %bitcast.7, f32[1,4096]{1,0:T(1,128)} %bitcast.8, s32[1]{0:T(128)S(6)} %copy.13.count_ref), custom_call_target="tpu_custom_call" | custom-call | tf_op jit(solution)/shard_map/residual/pallas_call | solution.py:386
  53.7 23.3 %back.1 = f32[16,32768]{1,0:T(8,128)} custom-call(bf16[16,32768]{1,0:T(8,128)(2,1)} %bitcast.13, s32[1,12288]{1,0:T(1,128)} %cells.1.cell_ref, f32[1,12288]{1,0:T(1,128)} %residual.1.v_ref, bf16[128,128]{1,0:T(8,128)(2,1)} %constant.10.clone.kz_ref, bf16[256,1536]{1,0:T(8,128)(2,1)} %constant.11.clone.ky_ref, bf16[3,16,16]{2,1,0:T(8,128)(2,1)} %constant.13.clone.kx_ref), custom_call_target="tpu_custom_call" | custom-call | flops 12884901888 | bytes 3145728 | tf_op jit(solution)/shard_map/back/pallas_call | solution.py:398
